TPU v7x, 128 devices: a whole 4x4x4 slice. The times are simulated.
128 devices in a mesh: row: 16 (over z, x_lo, core), col: 8 (over y, x_hi).
Axes of the slice: x: 4 (x_hi: 2, x_lo: 2; x = x_hi * 2 + x_lo), y: 4, z: 4, core: 2. Of those that a mesh axis runs over, the one named last changes fastest.
Arguments:
- image_emb: bfloat16 [16384, 1152], P(('row', 'col')), may hold values from -0.5 to 0.5, as said below
- text_emb: bfloat16 [16384, 1152], P(('col', 'row')), may hold values from -0.5 to 0.5, as said below
- scale: float32 [1], replicated, may hold values from 10 to 40
- bias: float32 [1], replicated, may hold values from -10 to -4
Outputs:
- grad_image: float32 [16384, 1152], P(('row', 'col'))
- grad_text: float32 [16384, 1152], P(('col', 'row'))
Inputs may be any that keep to these rules, and one draw needn't show every extreme that they name: `image_emb`: raw tower outputs; the image and the text of the same index form a matching pair. `text_emb`: raw tower outputs, paired with image_emb by index.
All inputs are finite; a program needn't handle non-finite values.
Results may differ from a plain program's by a relative error of at most 0.0086.
Values may be sent and summed in bfloat16 or wider, within the bound.
A program may use at most 64 MiB of HBM per device.

v0:
```python
import math

import jax
import jax.numpy as jnp
from jax import lax
from jax.sharding import PartitionSpec as P


def unit_rows(raw):
    values = raw.astype(jnp.float32)
    inverse = lax.rsqrt(jnp.sum(values * values, axis=1, keepdims=True) + 1e-06)
    return (inverse, values * inverse)


def tile_terms(img_unit, txt_unit, img_start, txt_start, scale_value, bias_value):
    sims = lax.dot_general(
        img_unit, txt_unit, (((1,), (1,)), ((), ())), preferred_element_type=jnp.float32
    )
    logits = scale_value * sims + bias_value
    rows = img_start + lax.broadcasted_iota(jnp.int32, sims.shape, 0)
    cols = txt_start + lax.broadcasted_iota(jnp.int32, sims.shape, 1)
    sign = jnp.where(rows == cols, 1.0, -1.0).astype(jnp.float32)
    coef = (-scale_value * sign * jax.nn.sigmoid(-sign * logits)).astype(jnp.bfloat16)
    g_img = jnp.dot(coef, txt_unit, preferred_element_type=jnp.float32)
    g_txt = lax.dot_general(
        coef, img_unit, (((0,), (0,)), ((), ())), preferred_element_type=jnp.float32
    )
    return (g_img, g_txt)


def finish(inverse, normed, grads):
    return inverse * (grads - normed * jnp.sum(normed * grads, axis=1, keepdims=True))


def per_device(image_emb, text_emb, scale, bias):
    img_inv, img_norm = unit_rows(image_emb)
    txt_inv, txt_norm = unit_rows(text_emb)
    img_unit = img_norm.astype(jnp.bfloat16)
    txt_unit = txt_norm.astype(jnp.bfloat16)
    shard_rows = image_emb.shape[0]
    width = image_emb.shape[1]
    row_count = lax.axis_size("row")
    col_count = lax.axis_size("col")
    scale_value = scale[0]
    bias_value = bias[0]
    img_block = lax.all_gather(img_unit, "col", axis=0, tiled=True)
    img_start = lax.axis_index("row") * (shard_rows * col_count)
    txt_base = lax.axis_index("col") * (shard_rows * row_count)
    txt_block = lax.all_gather(txt_unit, "row", axis=0, tiled=True)
    txt_rows = txt_block.shape[0]
    cols_step = math.gcd(512, txt_rows)

    def sweep(index, carry):
        g_img, g_txt = carry
        start = index * cols_step
        piece = lax.dynamic_slice_in_dim(txt_block, start, cols_step, 0)
        g_piece, t_piece = tile_terms(
            img_block, piece, img_start, txt_base + start, scale_value, bias_value
        )
        g_txt = lax.dynamic_update_slice_in_dim(g_txt, t_piece, start, 0)
        return (g_img + g_piece, g_txt)

    init = (
        jnp.zeros((img_block.shape[0], width), jnp.float32),
        jnp.zeros((txt_rows, width), jnp.float32),
    )
    g_img_part, g_txt_part = lax.fori_loop(0, txt_rows // cols_step, sweep, init)
    g_txt = lax.psum_scatter(g_txt_part, "row", scatter_dimension=0, tiled=True)
    g_img = lax.psum_scatter(g_img_part, "col", scatter_dimension=0, tiled=True)
    grad_image = finish(img_inv, img_norm, g_img)
    grad_text = finish(txt_inv, txt_norm, g_txt)
    return (grad_image, grad_text)


def solution(mesh):
    placed = (P(("row", "col"), None), P(("col", "row"), None), P(), P())
    return jax.shard_map(
        per_device,
        mesh=mesh,
        in_specs=placed,
        out_specs=(P(("row", "col"), None), P(("col", "row"), None)),
        check_vma=False,
    )
```

profile of v0, /device:TPU:8, one launch (start us, length us, event | category | flops | bytes accessed | tf_op | source)
XLA Modules:
  0.0 366.7 jit_solution(9852510663837325972)
XLA Ops:
  7.2 0.0 all-gather.5.cloned.1.call-start
  7.2 1.1 fusion.20
  8.3 1.8 fusion.16
  10.1 0.0 all-gather.5.cloned.1.call-update
  10.1 0.0 all-gather.3.cloned.1.call-start
  10.2 1.1 fusion.24
  11.3 1.8 fusion.13
  13.1 0.0 all-gather.3.cloned.1.call-update
  13.1 0.0 reduce-scatter.3.cloned.1.call-start
  13.8 54.0 %all-gather.5.cloned.1.call-done = bf16[1024,1152]{1,0:T(8,128)(2,1)} async-done(((bf16[128,1152]{1,0:T(8,128)(2,1)}), bf16[1024,1152]{1,0:T(8,128)(2,1)}) %all-gather.5.cloned.1.call-update) | async-done | bytes 2359312 | tf_op jit(solution)/shard_map/all_gather | solution.py:46
  67.9 40.1 %all-gather.3.cloned.1.call-done = bf16[2048,1152]{1,0:T(8,128)(2,1)} async-done(((bf16[128,1152]{1,0:T(8,128)(2,1)}), bf16[2048,1152]{1,0:T(8,128)(2,1)}) %all-gather.3.cloned.1.call-update) | async-done | bytes 4718608 | tf_op jit(solution)/shard_map/all_gather | solution.py:49
  108.0 4.2 %broadcast_in_dim.29 = f32[2048,1152]{1,0:T(8,128)} broadcast(f32[]{:T(128)} %constant.62.clone.1), dimensions={} | broadcast | bytes 9437188 | tf_op jit(solution)/shard_map/broadcast_in_dim | solution.py:65
  112.2 0.0 copy-done.4
  112.2 47.5 %while.17 = (s32[]{:T(128)}, f32[1024,1152]{1,0:T(8,128)}, f32[2048,1152]{1,0:T(8,128)}, f32[]{:T(128)}, s32[]{:T(128)}, /*index=5*/s32[]{:T(128)}, f32[]{:T(128...) while((s32[]{:T(128)}, f32[1024,1152]{1,0:T(8,128)}, ...), condition=%wide.region_3.4_spmd.clone, body=%wide.region_2.3_spmd.clone.sunk | while | flops 3632530944 | bytes 59782940 | solution.py:67
  112.2 0.0 copy-start
  112.2 4.9 %fusion.42 = bf16[1024,512]{0,1:T(8,128)(2,1)S(1)} fusion(bf16[1024,1152]{1,0:T(8,128)(2,1)S(1)} %get-tuple-element.350, f32[]{:T(128)} %get-tuple-element.351, f32[]{:T(128)} %get-tuple-element.348, s32[1024]{0:T(1024)S(1)} %iota_add_fusion.4, f32[]{:T(128)} %get-tuple-element.345, s32[512]{0:T(512)S(1)} %iota_add_fusion.5, ...), kind=kOutput, calls=%fused_computation.5.clone.1 | convolution fusion | flops 1214251008 | bytes 4595204 | tf_op jit(solution)/shard_map/while/body/eval_jaxpr/dot_general | solution.py:16
  117.2 0.0 copy-done
  117.2 3.9 %convolution_add_fusion.2 = f32[1024,1152]{1,0:T(8,128)S(1)} fusion(bf16[1024,512]{0,1:T(8,128)(2,1)S(1)} %fusion.42, f32[1024,1152]{1,0:T(8,128)S(1)} %copy-done, pred[]{:T(512)S(6)} %compare.3, bf16[2048,1152]{1,0:T(8,128)(2,1)} %get-tuple-element.349, s32[]{:T(128)S(6)} %select_n.41), kind=kOutput, calls=%fused_computation.clone.1 | convolution fusion | flops 1210318848 | bytes 11665413 | tf_op jit(solution)/shard_map/while/body/eval_jaxpr/dot_general | solution.py:24
  121.1 0.0 copy-start.1
  121.1 3.0 convolution_dynamic-update-slice_fusion.2
  124.1 0.0 copy-done.1
  124.1 0.0 copy-start
  124.1 4.9 %fusion.42 = bf16[1024,512]{0,1:T(8,128)(2,1)S(1)} fusion(bf16[1024,1152]{1,0:T(8,128)(2,1)S(1)} %get-tuple-element.350, f32[]{:T(128)} %get-tuple-element.351, f32[]{:T(128)} %get-tuple-element.348, s32[1024]{0:T(1024)S(1)} %iota_add_fusion.4, f32[]{:T(128)} %get-tuple-element.345, s32[512]{0:T(512)S(1)} %iota_add_fusion.5, ...), kind=kOutput, calls=%fused_computation.5.clone.1 | convolution fusion | flops 1214251008 | bytes 4595204 | tf_op jit(solution)/shard_map/while/body/eval_jaxpr/dot_general | solution.py:16
  129.0 0.0 copy-done
  129.1 3.9 %convolution_add_fusion.2 = f32[1024,1152]{1,0:T(8,128)S(1)} fusion(bf16[1024,512]{0,1:T(8,128)(2,1)S(1)} %fusion.42, f32[1024,1152]{1,0:T(8,128)S(1)} %copy-done, pred[]{:T(512)S(6)} %compare.3, bf16[2048,1152]{1,0:T(8,128)(2,1)} %get-tuple-element.349, s32[]{:T(128)S(6)} %select_n.41), kind=kOutput, calls=%fused_computation.clone.1 | convolution fusion | flops 1210318848 | bytes 11665413 | tf_op jit(solution)/shard_map/while/body/eval_jaxpr/dot_general | solution.py:24
  133.0 0.0 copy-start.1
  133.0 2.9 convolution_dynamic-update-slice_fusion.2
  135.9 0.0 copy-done.1
  135.9 0.0 copy-start
  135.9 4.9 %fusion.42 = bf16[1024,512]{0,1:T(8,128)(2,1)S(1)} fusion(bf16[1024,1152]{1,0:T(8,128)(2,1)S(1)} %get-tuple-element.350, f32[]{:T(128)} %get-tuple-element.351, f32[]{:T(128)} %get-tuple-element.348, s32[1024]{0:T(1024)S(1)} %iota_add_fusion.4, f32[]{:T(128)} %get-tuple-element.345, s32[512]{0:T(512)S(1)} %iota_add_fusion.5, ...), kind=kOutput, calls=%fused_computation.5.clone.1 | convolution fusion | flops 1214251008 | bytes 4595204 | tf_op jit(solution)/shard_map/while/body/eval_jaxpr/dot_general | solution.py:16
  140.9 0.0 copy-done
  140.9 3.9 %convolution_add_fusion.2 = f32[1024,1152]{1,0:T(8,128)S(1)} fusion(bf16[1024,512]{0,1:T(8,128)(2,1)S(1)} %fusion.42, f32[1024,1152]{1,0:T(8,128)S(1)} %copy-done, pred[]{:T(512)S(6)} %compare.3, bf16[2048,1152]{1,0:T(8,128)(2,1)} %get-tuple-element.349, s32[]{:T(128)S(6)} %select_n.41), kind=kOutput, calls=%fused_computation.clone.1 | convolution fusion | flops 1210318848 | bytes 11665413 | tf_op jit(solution)/shard_map/while/body/eval_jaxpr/dot_general | solution.py:24
  144.8 3.0 convolution_dynamic-update-slice_fusion.2
  147.8 4.9 %fusion.42 = bf16[1024,512]{0,1:T(8,128)(2,1)S(1)} fusion(bf16[1024,1152]{1,0:T(8,128)(2,1)S(1)} %get-tuple-element.350, f32[]{:T(128)} %get-tuple-element.351, f32[]{:T(128)} %get-tuple-element.348, s32[1024]{0:T(1024)S(1)} %iota_add_fusion.4, f32[]{:T(128)} %get-tuple-element.345, s32[512]{0:T(512)S(1)} %iota_add_fusion.5, ...), kind=kOutput, calls=%fused_computation.5.clone.1 | convolution fusion | flops 1214251008 | bytes 4595204 | tf_op jit(solution)/shard_map/while/body/eval_jaxpr/dot_general | solution.py:16
  152.8 3.9 %convolution_add_fusion.2 = f32[1024,1152]{1,0:T(8,128)S(1)} fusion(bf16[1024,512]{0,1:T(8,128)(2,1)S(1)} %fusion.42, f32[1024,1152]{1,0:T(8,128)S(1)} %copy-done, pred[]{:T(512)S(6)} %compare.3, bf16[2048,1152]{1,0:T(8,128)(2,1)} %get-tuple-element.349, s32[]{:T(128)S(6)} %select_n.41), kind=kOutput, calls=%fused_computation.clone.1 | convolution fusion | flops 1210318848 | bytes 11665413 | tf_op jit(solution)/shard_map/while/body/eval_jaxpr/dot_general | solution.py:24
  156.7 3.0 convolution_dynamic-update-slice_fusion.2
  159.7 0.0 copy-done.1
  159.7 0.0 reduce-scatter.3.cloned.1.call-update
  159.7 0.0 reduce-scatter.5.cloned.1.call-start
  159.8 0.0 copy-start.2
  159.8 0.5 reduce-scatter.5.cloned.1.call-update
  160.3 0.0 copy-start.3
  160.3 86.5 %reduce-scatter.3.cloned.1.call-done = f32[128,1152]{1,0:T(8,128)} async-done(((f32[1024,1152]{1,0:T(8,128)}), f32[128,1152]{1,0:T(8,128)}) %reduce-scatter.3.cloned.1.call-update) | async-done | bytes 589840 | tf_op jit(solution)/shard_map/reduce_scatter | solution.py:69
  246.8 1.3 fusion.17
  248.1 2.1 fusion.19
  250.2 106.6 %reduce-scatter.5.cloned.1.call-done = f32[128,1152]{1,0:T(8,128)} async-done(((f32[2048,1152]{1,0:T(8,128)}), f32[128,1152]{1,0:T(8,128)}) %reduce-scatter.5.cloned.1.call-update) | async-done | bytes 589840 | tf_op jit(solution)/shard_map/reduce_scatter | solution.py:68
  356.8 1.3 fusion.21
  358.1 2.1 fusion.23
  (19 shorter events, 0.1 us)
Async XLA Ops:
  7.2 60.7 %all-gather.5.cloned.1.call-start = ((), (), s32[]{:S(2)}) async-start(), calls=%async_computation.3 | async-start | bytes 2654208 | tf_op jit(solution)/shard_map/all_gather | solution.py:46
  10.1 97.8 %all-gather.3.cloned.1.call-start = ((), (), s32[]{:S(2)}) async-start(), calls=%async_computation.2 | async-start | bytes 5013504 | tf_op jit(solution)/shard_map/all_gather | solution.py:49
  13.1 233.7 %reduce-scatter.3.cloned.1.call-start = ((), (), s32[]{:S(2)}) async-start(), calls=%async_computation.4 | async-start | bytes 5308416 | tf_op jit(solution)/shard_map/reduce_scatter | solution.py:69
  108.0 4.2 %copy-start.4 = (bf16[1024,1152]{1,0:T(8,128)(2,1)S(1)}, bf16[1024,1152]{1,0:T(8,128)(2,1)}, u32[]{:S(2)}) copy-start(bf16[1024,1152]{1,0:T(8,128)(2,1)} %all-gather.5.cloned.1.call-done) | copy-start | bytes 7077892
  112.2 5.0 %copy-start = (f32[1024,1152]{1,0:T(8,128)S(1)}, f32[1024,1152]{1,0:T(8,128)}, u32[]{:S(2)}) copy-start(f32[1024,1152]{1,0:T(8,128)} %get-tuple-element.329) | copy-start | bytes 14155780 | tf_op jit(solution)/shard_map/while
  121.1 3.0 copy-start.1
  124.1 5.0 %copy-start = (f32[1024,1152]{1,0:T(8,128)S(1)}, f32[1024,1152]{1,0:T(8,128)}, u32[]{:S(2)}) copy-start(f32[1024,1152]{1,0:T(8,128)} %get-tuple-element.329) | copy-start | bytes 14155780 | tf_op jit(solution)/shard_map/while
  133.0 3.0 copy-start.1
  135.9 5.0 %copy-start = (f32[1024,1152]{1,0:T(8,128)S(1)}, f32[1024,1152]{1,0:T(8,128)}, u32[]{:S(2)}) copy-start(f32[1024,1152]{1,0:T(8,128)} %get-tuple-element.329) | copy-start | bytes 14155780 | tf_op jit(solution)/shard_map/while
  144.8 3.0 copy-start.1
  147.8 5.0 %copy-start = (f32[1024,1152]{1,0:T(8,128)S(1)}, f32[1024,1152]{1,0:T(8,128)}, u32[]{:S(2)}) copy-start(f32[1024,1152]{1,0:T(8,128)} %get-tuple-element.329) | copy-start | bytes 14155780 | tf_op jit(solution)/shard_map/while
  156.7 3.0 copy-start.1
  159.7 197.1 %reduce-scatter.5.cloned.1.call-start = ((), (), s32[]{:S(2)}) async-start(), calls=%async_computation.5 | async-start | bytes 10027008 | tf_op jit(solution)/shard_map/reduce_scatter | solution.py:68
  159.8 87.0 %copy-start.2 = (bf16[128,1152]{1,0:T(8,128)(2,1)S(1)}, bf16[128,1152]{1,0:T(8,128)(2,1)}, u32[]{:S(2)}) copy-start(bf16[128,1152]{1,0:T(8,128)(2,1)} %param.6) | copy-start | bytes 884740
  160.3 196.5 %copy-start.3 = (bf16[128,1152]{1,0:T(8,128)(2,1)S(1)}, bf16[128,1152]{1,0:T(8,128)(2,1)}, u32[]{:S(2)}) copy-start(bf16[128,1152]{1,0:T(8,128)(2,1)} %param.7) | copy-start | bytes 884740
Sparse Core Ops, SparseCore 0:
  10.9 56.9 all-gather.4
  70.1 37.7 all-gather.2
  159.9 86.8 reduce-scatter.2
  249.1 107.6 reduce-scatter.4
where the time goes:
time: 368 us; the launch traced here: 367 us
  waiting for transfers between devices  288 us (78%)
  matrix products  47.3 us (13%)
  between operations  14.4 us (4%)
  other arithmetic  12.6 us (3%)
  local copies, waits for them, and re-layouts  4.28 us (1%)
    reduce_scatter x1, waiting for transfers between devices, per_device(): g_txt = lax.psum_scatter(g_txt_part, 'row', scatter_dimension=0, tiled=True)  107 us
    reduce_scatter x1, waiting for transfers between devices, per_device(): g_img = lax.psum_scatter(g_img_part, 'col', scatter_dimension=0, tiled=True)  86.5 us
    all_gather x1, waiting for transfers between devices, per_device(): img_block = lax.all_gather(img_unit, 'col', axis=0, tiled=True)  54 us
    all_gather x1, waiting for transfers between devices, per_device(): txt_block = lax.all_gather(txt_unit, 'row', axis=0, tiled=True)  40.1 us
    dot_general x4, matrix products, tile_terms(): lax.dot_general(img_unit, txt_unit, (((1,), (1,)), ((), ())), preferred_e...  19.8 us
    dot_general x4, matrix products, tile_terms(): g_img = jnp.dot(coef, txt_unit, preferred_element_type=jnp.float32)  15.6 us
    dot_general x4, matrix products, tile_terms(): lax.dot_general(coef, img_unit, (((0,), (0,)), ((), ())), preferred_eleme...  11.9 us
  transfers between devices with their start and end apart: 4, of which 4 were waited for; matrix products, arithmetic and copies ran while one was open for 2% of the time, Pallas kernels for 0%

commit v1 on v0

v1 whole, which is shorter than its diff:
```python
import jax
import jax.numpy as jnp
from jax import lax
from jax.experimental import pallas as pl
from jax.experimental.pallas import tpu as pltpu
from jax.sharding import PartitionSpec as P

MESH = pl.DeviceIdType.MESH
F32 = jnp.float32
BF16 = jnp.bfloat16
SHARD = 128
PARTS = ((0, 48), (48, 48), (96, 32))
ORDER = (0, 2, 1, 3, 5, 7, 4, 6)
SLOT = {position: slot for slot, position in enumerate(ORDER)}


def dot(a, b, contract):
    return lax.dot_general(a, b, (contract, ((), ())), preferred_element_type=F32)


def unit_rows(raw):
    values = raw.astype(F32)
    inverse = lax.rsqrt(jnp.sum(values * values, axis=1, keepdims=True) + 1e-06)
    return (inverse, values * inverse)


def low_bit(position):
    return next(s for s in range(3) if position >> s & 1)


def high_bit(position):
    return max(s for s in range(3) if position >> s & 1)


class Place:
    def __init__(self):
        row, col = lax.axis_index("row"), lax.axis_index("col")
        self.core = lax.rem(row, 2)
        x = lax.rem(col, 2) * 2 + lax.rem(lax.div(row, 2), 2)
        self.chip = (x, lax.div(col, 2), lax.div(row, 4))
        even = tuple(c + 1 - 2 * lax.rem(c, 2) for c in self.chip)
        odd = tuple(lax.rem(c + 3 + 2 * lax.rem(c, 2), 4) for c in self.chip)
        self.partner = (even, odd)

    def device(self, chip, core):
        x, y, z = chip
        return (z * 4 + lax.rem(x, 2) * 2 + core, y * 2 + lax.div(x, 2))

    def sibling(self):
        return self.device(self.chip, 1 - self.core)

    def neighbour(self, kind, axis):
        chip = list(self.chip)
        chip[axis] = self.partner[kind][axis]
        return self.device(chip, self.core)

    def along(self, kind, part, step):
        a = self.neighbour(kind, (part + step) % 3)
        b = self.neighbour(kind, (part + step + 1) % 3)
        return tuple(u + self.core * (v - u) for u, v in zip(a, b))

    def shard(self, kind, part, position, core):
        chip = []
        for axis in range(3):
            f0 = position >> ((axis - part) % 3) & 1
            f1 = position >> ((axis - part - 1) % 3) & 1
            flip = f0 + core * (f1 - f0)
            chip.append(self.chip[axis] + flip * (self.partner[kind][axis] - self.chip[axis]))
        row, col = self.device(chip, core)
        return row * 8 + col if kind == 0 else col * 16 + row


def kernel(
    scale_ref, bias_ref, image_ref, text_ref, grad_image_ref, grad_text_ref,
    img, txt, g_img, g_txt, img_out, img_in, txt_out, txt_in, sib_out, sib_in, img_id, txt_id,
    gather_send, gather_recv, pair_send, pair_recv, reduce_send, reduce_recv, back_send, back_recv,
):
    place = Place()
    sibling = place.sibling()
    links = [place.neighbour(kind, axis) for kind in range(2) for axis in range(3)]
    hops = [[[place.along(kind, p, s) for s in range(3)] for p in range(3)] for kind in range(2)]

    barrier = pltpu.get_barrier_semaphore()
    for other in links + [sibling]:
        pl.semaphore_signal(barrier, inc=1, device_id=other, device_id_type=MESH)

    image_inverse, image_norm = unit_rows(image_ref[...])
    img[0:SHARD, :] = image_norm.astype(BF16)
    text_inverse, text_norm = unit_rows(text_ref[...])
    txt[0:SHARD, :] = text_norm.astype(BF16)
    scale = scale_ref[0]
    bias = bias_ref[0]

    pl.semaphore_wait(barrier, len(links) + 1)

    held = (img, txt)
    outs, ins = (img_out, txt_out), (img_in, txt_in)
    stride = (SHARD, 2 * SHARD)

    def rows(ref, kind, position, part=None, side=0, step=None):
        first = SLOT[position] * (stride[kind] if step is None else step) + side * SHARD
        if part is None:
            return ref.at[pl.ds(first, SHARD)]
        return ref.at[pl.ds(first + PARTS[part][0], PARTS[part][1])]

    def remote(src, dst, send, recv, device):
        return pltpu.make_async_remote_copy(
            src_ref=src, dst_ref=dst, send_sem=send, recv_sem=recv, device_id=device, device_id_type=MESH
        )

    def pass_on(kind, position, step):
        target = position + (1 << step)
        for p in range(3):
            remote(
                rows(held[kind], kind, position, p), rows(held[kind], kind, target, p),
                gather_send.at[kind, target], gather_recv.at[kind, target], hops[kind][p][step],
            ).start()

    def gathered(kind, position):
        whole = rows(held[kind], kind, position)
        return remote(whole, whole, gather_send.at[kind, position], gather_recv.at[kind, position], sibling)

    def pair_copy(position):
        return remote(
            rows(txt, 1, position), rows(txt, 1, position, side=1),
            pair_send.at[position], pair_recv.at[position], sibling,
        )

    def reduced(kind, position):
        return remote(
            rows(outs[kind], kind, position, step=SHARD), rows(ins[kind], kind, position, step=SHARD),
            reduce_send.at[kind, position], reduce_recv.at[kind, position], sibling,
        )

    def back_copy(position):
        return remote(
            rows(sib_out, 1, position, step=SHARD), rows(sib_in, 1, position, step=SHARD),
            back_send.at[position], back_recv.at[position], sibling,
        )

    for step in (0, 1):
        for kind in (0, 1):
            pass_on(kind, 0, step)
    pair_copy(0).start()

    g_img[...] = jnp.zeros_like(g_img)
    g_txt[...] = jnp.zeros_like(g_txt)
    down = lax.broadcasted_iota(jnp.int32, (SHARD, 128), 0)
    across = lax.broadcasted_iota(jnp.int32, (8, SHARD), 1)

    def numbers(index, kind, position, core):
        a, b, c = (place.shard(kind, p, position, core) * SHARD for p in range(3))
        return index + jnp.where(index < PARTS[1][0], a, jnp.where(index < PARTS[2][0], b, c))

    for position in range(8):
        first = SLOT[position] * SHARD
        img_id[first : first + SHARD, :] = numbers(down, 0, position, place.core)
        for side, core in enumerate((place.core, 1 - place.core)):
            begin = SLOT[position] * 2 * SHARD + side * SHARD
            txt_id[:, begin : begin + SHARD] = numbers(across, 1, position, core)

    for kind in (0, 1):
        gathered(kind, 1).wait_recv()
        pass_on(kind, 1, 1)
    for kind in (0, 1):
        pass_on(kind, 1, 2)
    pair_copy(1).start()
    for position in (3, 2):
        for kind in (1, 0):
            gathered(kind, position).wait_recv()
        for kind in (1, 0):
            pass_on(kind, position, 2)
            if position == 3:
                pass_on(kind, 0, 2)
        pair_copy(position).start()

    def block(a, a_count, b):
        r = pl.ds(a * 2 * SHARD, a_count * 2 * SHARD)
        c = pl.ds(b * 4 * SHARD, 4 * SHARD)
        sims = dot(img[r, :], txt[c, :], ((1,), (1,)))
        same = img_id[r, 0:1] == txt_id[0:1, c]
        logits = scale * sims + bias
        coef = scale / (1.0 + jnp.exp(jnp.where(same, logits, -logits)))
        coef = jnp.where(same, -coef, coef).astype(BF16)
        g_img[r, :] += dot(coef, txt[c, :], ((1,), (0,)))
        g_txt[c, :] += dot(coef, img[r, :], ((0,), (0,)))

    def paired(*positions):
        for position in positions:
            pair_copy(position).wait_recv()

    def arrive(kind, *positions):
        for position in positions:
            gathered(kind, position).wait_recv()
            if kind == 1:
                pair_copy(position).start()

    def give_back(*positions):
        for position in positions:
            other = rows(g_txt, 1, position, side=1)
            rows(sib_out, 1, position, step=SHARD)[...] = other[...].astype(BF16)
            back_copy(position).start()

    def total(kind, position):
        value = rows((g_img, g_txt)[kind], kind, position)[...]
        if kind == 1:
            back_copy(position).wait_recv()
            value += rows(sib_in, 1, position, step=SHARD)[...].astype(F32)
        for s in range(3 if position == 0 else low_bit(position)):
            child = position + (1 << s)
            reduced(kind, child).wait_recv()
            value += rows(ins[kind], kind, child, step=SHARD)[...].astype(F32)
        return value

    def hand_on(kind, *positions):
        for position in positions:
            rows(outs[kind], kind, position, step=SHARD)[...] = total(kind, position).astype(BF16)
            for p in range(3):
                remote(
                    rows(outs[kind], kind, position, p, step=SHARD), rows(ins[kind], kind, position, p, step=SHARD),
                    reduce_send.at[kind, position], reduce_recv.at[kind, position],
                    hops[kind][p][low_bit(position)],
                ).start()

    paired(0, 2)
    block(0, 2, 0)
    arrive(1, 5)
    paired(1, 3)
    block(0, 2, 1)
    arrive(1, 7)
    arrive(0, 5, 7)
    block(2, 1, 0)
    arrive(1, 4)
    paired(5, 7)
    block(0, 2, 2)
    arrive(1, 6)
    arrive(0, 4, 6)
    block(2, 2, 1)
    give_back(1, 3)
    block(2, 2, 2)
    give_back(5, 7)
    hand_on(1, 1, 3)
    paired(4, 6)
    block(1, 2, 3)
    hand_on(1, 5, 7)
    hand_on(0, 1, 3, 5, 7)
    block(3, 1, 3)
    block(0, 1, 3)
    give_back(6, 4)
    block(3, 1, 0)
    give_back(2, 0)
    hand_on(1, 6)
    hand_on(0, 6)
    hand_on(1, 2)
    hand_on(0, 2)
    hand_on(1, 4)
    hand_on(0, 4)

    def finish(inverse, normed, grads):
        return inverse * (grads - normed * jnp.sum(normed * grads, axis=1, keepdims=True))

    text_inverse, text_norm = unit_rows(text_ref[...])
    grad_text_ref[...] = finish(text_inverse, text_norm, total(1, 0))
    image_inverse, image_norm = unit_rows(image_ref[...])
    grad_image_ref[...] = finish(image_inverse, image_norm, total(0, 0))

    for position in range(8):
        pair_copy(position).wait_send()
        back_copy(position).wait_send()
        if position:
            for kind in (0, 1):
                gathered(kind, position).wait_send()
                reduced(kind, position).wait_send()


def per_device(image_emb, text_emb, scale, bias):
    width = image_emb.shape[1]
    vmem = pl.BlockSpec(memory_space=pltpu.VMEM)
    smem = pl.BlockSpec(memory_space=pltpu.SMEM)
    dma = pltpu.SemaphoreType.DMA
    whole = 8 * SHARD
    out = jax.ShapeDtypeStruct((SHARD, width), F32)
    return pl.pallas_call(
        kernel,
        out_shape=(out, out),
        in_specs=[smem, smem, vmem, vmem],
        out_specs=(vmem, vmem),
        scratch_shapes=[
            pltpu.VMEM((whole, width), BF16),
            pltpu.VMEM((2 * whole, width), BF16),
            pltpu.VMEM((whole, width), F32),
            pltpu.VMEM((2 * whole, width), F32),
            *[pltpu.VMEM((whole, width), BF16) for _ in range(6)],
            pltpu.VMEM((whole, 128), jnp.int32),
            pltpu.VMEM((8, 2 * whole), jnp.int32),
            dma((2, 8)), dma((2, 8)), dma((8,)), dma((8,)),
            dma((2, 8)), dma((2, 8)), dma((8,)), dma((8,)),
        ],
        compiler_params=pltpu.CompilerParams(
            collective_id=0, has_side_effects=True, vmem_limit_bytes=60 * 2**20
        ),
        cost_estimate=pl.CostEstimate(
            flops=6 * 2 * whole * whole * width, bytes_accessed=12 * SHARD * width, transcendentals=2 * whole * whole
        ),
    )(scale, bias, image_emb, text_emb)


def solution(mesh):
    placed = (P(("row", "col"), None), P(("col", "row"), None), P(), P())
    return jax.shard_map(
        per_device,
        mesh=mesh,
        in_specs=placed,
        out_specs=(P(("row", "col"), None), P(("col", "row"), None)),
        check_vma=False,
    )
```

time: 368 us -> 63.6 us (0.17)
  waiting for transfers between devices: 288 us -> 0 us
  Pallas kernels: 0 us -> 58.7 us
  matrix products: 47.3 us -> 0 us
  other arithmetic: 12.6 us -> 0 us
  between operations: 14.4 us -> 1.94 us
    reduce_scatter x2 -> x0, waiting for transfers between devices: 193 us -> none  [the longest x1 107 us: per_device(): g_txt = lax.psum_scatter(g_txt_part, 'row', scatter_dimension=0, tiled=True)]
    all_gather x2 -> x0, waiting for transfers between devices: 94.1 us -> none  [the longest x1 54 us: per_device(): img_block = lax.all_gather(img_unit, 'col', axis=0, tiled=True)]
    pallas_call x0 -> x1, Pallas kernels: none -> 58.7 us  [per_device(): pl.pallas_call(kernel, out_shape=(out, out), in_specs=[smem, smem, vmem,...]
    dot_general x12 -> x0, matrix products: 47.3 us -> none  [the longest x4 19.8 us: tile_terms(): lax.dot_general(img_unit, txt_unit, (((1,), (1,)), ((), ())), preferred_e...]
    reduce_sum x4 -> x0, other arithmetic: 4.78 us -> none  [the longest x2 2.58 us: finish(): jnp.sum(normed * grads, axis=1, keepdims=True)]
    broadcast_in_dim x1 -> x0, local copies, waits for them, and re-layouts: 4.23 us -> none  [per_device(): jnp.zeros((txt_rows, width), jnp.float32)]
    mul x2 -> x0, other arithmetic: 4.17 us -> none  [finish(): inverse * (grads - normed * jnp.sum(normed * grads, axis=1, keepdims=True))]
  transfers between devices with their start and end apart: 4 -> 0, of which waited for: 4 -> 0; matrix products, arithmetic and copies ran while one was open for 2% -> 0% of each run, Pallas kernels for 0% -> 0%
where the time goes in v1:
time: 63.6 us; the launch traced here: 63.4 us
  Pallas kernels  58.7 us (92%)
  local copies, waits for them, and re-layouts  2.8 us (4%)
  between operations  1.94 us (3%)
    pallas_call x1, Pallas kernels, per_device(): pl.pallas_call(kernel, out_shape=(out, out), in_specs=[smem, smem, vmem,...  58.7 us
    unnamed x4, local copies, waits for them, and re-layouts  2.8 us

profile of v1, /device:TPU:8, one launch (start us, length us, event | category | flops | bytes accessed | tf_op | source)
XLA Modules:
  0.0 63.4 jit_solution(14725802324238977321)
XLA Ops:
  1.9 58.7 %shard_map.59 = (f32[128,1152]{1,0:T(8,128)}, f32[128,1152]{1,0:T(8,128)}) custom-call(f32[1]{0:T(128)S(6)} %copy.8.scale_ref, f32[1]{0:T(128)S(6)} %copy.9.bias_ref, bf16[128,1152]{1,0:T(8,128)(2,1)} %image_ref.1, bf16[128,1152]{1,0:T(8,128)(2,1)} %text_ref.1), custom_call_target="tpu_custom_call" | custom-call | flops 14495514624 | bytes 1769472 | tf_op jit(solution)/shard_map/pallas_call | solution.py:283
  60.6 0.0 copy-start
  60.6 2.0 %copy.10 = f32[128,1152]{1,0:T(8,128)} copy(f32[128,1152]{1,0:T(8,128)} %get-tuple-element.4) | data formatting | bytes 1179648
  62.6 0.0 copy-done
  62.6 0.8 %copy.11 = f32[128,1152]{1,0:T(8,128)} copy(f32[128,1152]{1,0:T(8,128)S(1)} %copy-done) | data formatting | bytes 1179648
Async XLA Ops:
  60.6 2.0 %copy-start = (f32[128,1152]{1,0:T(8,128)S(1)}, f32[128,1152]{1,0:T(8,128)}, u32[]{:S(2)}) copy-start(f32[128,1152]{1,0:T(8,128)} %get-tuple-element.5) | copy-start | bytes 1769476

commit v2 on v1

--- a/solution.py
+++ b/solution.py
@@ -10,7 +10,7 @@
 BF16 = jnp.bfloat16
 SHARD = 128
 PARTS = ((0, 48), (48, 48), (96, 32))
-ORDER = (0, 2, 1, 3, 5, 7, 4, 6)
+ORDER = (0, 4, 1, 2, 3, 5, 6, 7)
 SLOT = {position: slot for slot, position in enumerate(ORDER)}
 
 
@@ -30,6 +30,13 @@
 
 def high_bit(position):
     return max(s for s in range(3) if position >> s & 1)
+
+
+def text_row(position, side):
+    slot = SLOT[position]
+    if slot < 4:
+        return (side * 4 + slot) * SHARD
+    return (slot // 2 * 4 + side * 2 + slot % 2) * SHARD
 
 
 class Place:
@@ -71,34 +78,32 @@
 
 
 def kernel(
-    scale_ref, bias_ref, image_ref, text_ref, grad_image_ref, grad_text_ref,
-    img, txt, g_img, g_txt, img_out, img_in, txt_out, txt_in, sib_out, sib_in, img_id, txt_id,
+    scale_hbm, bias_hbm, image_hbm, text_hbm, grad_image_ref, grad_text_ref,
+    scale_ref, bias_ref, image_ref, text_ref, load, img, txt, g_img, g_txt, img_out, img_in, txt_out, txt_in, sib_out, sib_in, img_id, txt_id,
     gather_send, gather_recv, pair_send, pair_recv, reduce_send, reduce_recv, back_send, back_recv,
 ):
     place = Place()
     sibling = place.sibling()
     links = [place.neighbour(kind, axis) for kind in range(2) for axis in range(3)]
-    hops = [[[place.along(kind, p, s) for s in range(3)] for p in range(3)] for kind in range(2)]
-
     barrier = pltpu.get_barrier_semaphore()
     for other in links + [sibling]:
         pl.semaphore_signal(barrier, inc=1, device_id=other, device_id_type=MESH)
 
-    image_inverse, image_norm = unit_rows(image_ref[...])
-    img[0:SHARD, :] = image_norm.astype(BF16)
-    text_inverse, text_norm = unit_rows(text_ref[...])
-    txt[0:SHARD, :] = text_norm.astype(BF16)
-    scale = scale_ref[0]
-    bias = bias_ref[0]
-
-    pl.semaphore_wait(barrier, len(links) + 1)
+    loads = [
+        pltpu.make_async_copy(src, dst, load.at[i])
+        for i, (src, dst) in enumerate(
+            ((image_hbm, image_ref), (text_hbm, text_ref), (scale_hbm, scale_ref), (bias_hbm, bias_ref))
+        )
+    ]
+    for copy in loads:
+        copy.start()
+    hops = [[[place.along(kind, p, s) for s in range(3)] for p in range(3)] for kind in range(2)]
 
     held = (img, txt)
     outs, ins = (img_out, txt_out), (img_in, txt_in)
-    stride = (SHARD, 2 * SHARD)
-
-    def rows(ref, kind, position, part=None, side=0, step=None):
-        first = SLOT[position] * (stride[kind] if step is None else step) + side * SHARD
+
+    def rows(ref, kind, position, part=None, side=0, packed=False):
+        first = SLOT[position] * SHARD if packed or kind == 0 else text_row(position, side)
         if part is None:
             return ref.at[pl.ds(first, SHARD)]
         return ref.at[pl.ds(first + PARTS[part][0], PARTS[part][1])]
@@ -128,20 +133,28 @@
 
     def reduced(kind, position):
         return remote(
-            rows(outs[kind], kind, position, step=SHARD), rows(ins[kind], kind, position, step=SHARD),
+            rows(outs[kind], kind, position, packed=True), rows(ins[kind], kind, position, packed=True),
             reduce_send.at[kind, position], reduce_recv.at[kind, position], sibling,
         )
 
     def back_copy(position):
         return remote(
-            rows(sib_out, 1, position, step=SHARD), rows(sib_in, 1, position, step=SHARD),
+            rows(sib_out, 1, position, packed=True), rows(sib_in, 1, position, packed=True),
             back_send.at[position], back_recv.at[position], sibling,
         )
 
-    for step in (0, 1):
-        for kind in (0, 1):
+    for kind, raw in ((1, text_ref), (0, image_ref)):
+        loads[kind].wait()
+        held[kind][0:SHARD, :] = unit_rows(raw[...])[1].astype(BF16)
+        if kind == 1:
+            pl.semaphore_wait(barrier, len(links) + 1)
+        for step in range(3):
             pass_on(kind, 0, step)
     pair_copy(0).start()
+    loads[2].wait()
+    loads[3].wait()
+    scale = scale_ref[0]
+    bias = bias_ref[0]
 
     g_img[...] = jnp.zeros_like(g_img)
     g_txt[...] = jnp.zeros_like(g_txt)
@@ -156,32 +169,27 @@
         first = SLOT[position] * SHARD
         img_id[first : first + SHARD, :] = numbers(down, 0, position, place.core)
         for side, core in enumerate((place.core, 1 - place.core)):
-            begin = SLOT[position] * 2 * SHARD + side * SHARD
+            begin = text_row(position, side)
             txt_id[:, begin : begin + SHARD] = numbers(across, 1, position, core)
 
-    for kind in (0, 1):
-        gathered(kind, 1).wait_recv()
-        pass_on(kind, 1, 1)
-    for kind in (0, 1):
-        pass_on(kind, 1, 2)
-    pair_copy(1).start()
-    for position in (3, 2):
+    for position in (1, 2):
         for kind in (1, 0):
             gathered(kind, position).wait_recv()
-        for kind in (1, 0):
-            pass_on(kind, position, 2)
-            if position == 3:
-                pass_on(kind, 0, 2)
+            for step in range(position, 3):
+                pass_on(kind, position, step)
         pair_copy(position).start()
+    for kind in (1, 0):
+        gathered(kind, 4).wait_recv()
+    pair_copy(4).start()
 
     def block(a, a_count, b):
         r = pl.ds(a * 2 * SHARD, a_count * 2 * SHARD)
         c = pl.ds(b * 4 * SHARD, 4 * SHARD)
         sims = dot(img[r, :], txt[c, :], ((1,), (1,)))
         same = img_id[r, 0:1] == txt_id[0:1, c]
-        logits = scale * sims + bias
-        coef = scale / (1.0 + jnp.exp(jnp.where(same, logits, -logits)))
-        coef = jnp.where(same, -coef, coef).astype(BF16)
+        odds = jnp.exp(-scale * sims - bias)
+        coef = scale / (1.0 + odds)
+        coef = (coef * jnp.where(same, -odds, 1.0)).astype(BF16)
         g_img[r, :] += dot(coef, txt[c, :], ((1,), (0,)))
         g_txt[c, :] += dot(coef, img[r, :], ((0,), (0,)))
 
@@ -192,67 +200,71 @@
     def arrive(kind, *positions):
         for position in positions:
             gathered(kind, position).wait_recv()
+            if position == 3:
+                pass_on(kind, 3, 2)
             if kind == 1:
                 pair_copy(position).start()
 
     def give_back(*positions):
         for position in positions:
             other = rows(g_txt, 1, position, side=1)
-            rows(sib_out, 1, position, step=SHARD)[...] = other[...].astype(BF16)
+            rows(sib_out, 1, position, packed=True)[...] = other[...].astype(BF16)
             back_copy(position).start()
 
     def total(kind, position):
         value = rows((g_img, g_txt)[kind], kind, position)[...]
         if kind == 1:
             back_copy(position).wait_recv()
-            value += rows(sib_in, 1, position, step=SHARD)[...].astype(F32)
+            value += rows(sib_in, 1, position, packed=True)[...].astype(F32)
         for s in range(3 if position == 0 else low_bit(position)):
             child = position + (1 << s)
             reduced(kind, child).wait_recv()
-            value += rows(ins[kind], kind, child, step=SHARD)[...].astype(F32)
+            value += rows(ins[kind], kind, child, packed=True)[...].astype(F32)
         return value
 
     def hand_on(kind, *positions):
         for position in positions:
-            rows(outs[kind], kind, position, step=SHARD)[...] = total(kind, position).astype(BF16)
+            rows(outs[kind], kind, position, packed=True)[...] = total(kind, position).astype(BF16)
             for p in range(3):
                 remote(
-                    rows(outs[kind], kind, position, p, step=SHARD), rows(ins[kind], kind, position, p, step=SHARD),
+                    rows(outs[kind], kind, position, p, packed=True), rows(ins[kind], kind, position, p, packed=True),
                     reduce_send.at[kind, position], reduce_recv.at[kind, position],
                     hops[kind][p][low_bit(position)],
                 ).start()
 
-    paired(0, 2)
     block(0, 2, 0)
+    arrive(1, 3)
+    arrive(0, 3)
+    paired(0, 1, 2, 4)
+    block(0, 2, 1)
     arrive(1, 5)
-    paired(1, 3)
-    block(0, 2, 1)
+    arrive(0, 5)
+    block(2, 1, 0)
+    block(2, 1, 1)
+    arrive(1, 6)
+    paired(3, 5)
+    block(0, 2, 2)
     arrive(1, 7)
-    arrive(0, 5, 7)
-    block(2, 1, 0)
-    arrive(1, 4)
-    paired(5, 7)
-    block(0, 2, 2)
-    arrive(1, 6)
-    arrive(0, 4, 6)
-    block(2, 2, 1)
-    give_back(1, 3)
+    arrive(0, 6, 7)
     block(2, 2, 2)
-    give_back(5, 7)
-    hand_on(1, 1, 3)
-    paired(4, 6)
-    block(1, 2, 3)
-    hand_on(1, 5, 7)
-    hand_on(0, 1, 3, 5, 7)
-    block(3, 1, 3)
-    block(0, 1, 3)
-    give_back(6, 4)
+    give_back(3, 5)
+    paired(6, 7)
+    block(0, 2, 3)
+    hand_on(0, 1)
+    hand_on(1, 3, 5)
+    block(2, 2, 3)
+    give_back(7, 6)
+    hand_on(0, 3, 5)
+    block(3, 1, 1)
+    give_back(1, 2, 4, 0)
+    hand_on(1, 7)
     block(3, 1, 0)
-    give_back(2, 0)
+    hand_on(0, 7)
+    hand_on(1, 1)
+    hand_on(0, 2)
+    hand_on(1, 2)
     hand_on(1, 6)
     hand_on(0, 6)
-    hand_on(1, 2)
-    hand_on(0, 2)
     hand_on(1, 4)
     hand_on(0, 4)
 
@@ -276,16 +288,20 @@
 def per_device(image_emb, text_emb, scale, bias):
     width = image_emb.shape[1]
     vmem = pl.BlockSpec(memory_space=pltpu.VMEM)
-    smem = pl.BlockSpec(memory_space=pltpu.SMEM)
     dma = pltpu.SemaphoreType.DMA
     whole = 8 * SHARD
     out = jax.ShapeDtypeStruct((SHARD, width), F32)
     return pl.pallas_call(
         kernel,
         out_shape=(out, out),
-        in_specs=[smem, smem, vmem, vmem],
+        in_specs=[pl.BlockSpec(memory_space=pl.ANY)] * 4,
         out_specs=(vmem, vmem),
         scratch_shapes=[
+            pltpu.SMEM((1,), F32),
+            pltpu.SMEM((1,), F32),
+            pltpu.VMEM((SHARD, width), BF16),
+            pltpu.VMEM((SHARD, width), BF16),
+            dma((4,)),
             pltpu.VMEM((whole, width), BF16),
             pltpu.VMEM((2 * whole, width), BF16),
             pltpu.VMEM((whole, width), F32),
@@ -297,7 +313,7 @@
             dma((2, 8)), dma((2, 8)), dma((8,)), dma((8,)),
         ],
         compiler_params=pltpu.CompilerParams(
-            collective_id=0, has_side_effects=True, vmem_limit_bytes=60 * 2**20
+            collective_id=0, has_side_effects=True, vmem_limit_bytes=50 * 2**20
         ),
         cost_estimate=pl.CostEstimate(
             flops=6 * 2 * whole * whole * width, bytes_accessed=12 * SHARD * width, transcendentals=2 * whole * whole

time: 63.6 us -> 58 us (0.912)
  Pallas kernels: 58.7 us -> 52.3 us
  local copies, waits for them, and re-layouts: 2.8 us -> 3.55 us
    pallas_call x1, Pallas kernels: 58.7 us -> 52.3 us  [per_device(): pl.pallas_call(kernel, out_shape=(out, out), in_specs=[pl.BlockSpec(memor...]
    unnamed x4 -> x6, local copies, waits for them, and re-layouts: 2.8 us -> 3.55 us
where the time goes in v2:
time: 58 us; the launch traced here: 57.8 us
  Pallas kernels  52.3 us (90%)
  local copies, waits for them, and re-layouts  3.55 us (6%)
  between operations  1.94 us (3%)
    pallas_call x1, Pallas kernels, per_device(): pl.pallas_call(kernel, out_shape=(out, out), in_specs=[pl.BlockSpec(memor...  52.3 us
    unnamed x6, local copies, waits for them, and re-layouts  3.55 us

profile of v2, /device:TPU:8, one launch (start us, length us, event | category | flops | bytes accessed | tf_op | source)
XLA Modules:
  0.0 57.8 jit_solution(12457442312661131995)
XLA Ops:
  1.9 0.0 copy-start
  1.9 1.0 %copy-done = bf16[128,1152]{1,0:T(8,128)(2,1)S(1)} copy-done((bf16[128,1152]{1,0:T(8,128)(2,1)S(1)}, bf16[128,1152]{1,0:T(8,128)(2,1)}, u32[]{:S(2)}) %copy-start) | copy-done | bytes 294936
  2.9 0.0 copy-start.1
  2.9 1.0 %copy-done.1 = bf16[128,1152]{1,0:T(8,128)(2,1)S(1)} copy-done((bf16[128,1152]{1,0:T(8,128)(2,1)S(1)}, bf16[128,1152]{1,0:T(8,128)(2,1)}, u32[]{:S(2)}) %copy-start.1) | copy-done | bytes 294936
  3.8 52.3 %shard_map.59 = (f32[128,1152]{1,0:T(8,128)S(1)}, f32[128,1152]{1,0:T(8,128)S(1)}) custom-call(f32[1]{0:T(128)S(6)} %copy.8.scale_hbm, f32[1]{0:T(128)S(6)} %copy.9.bias_hbm, bf16[128,1152]{1,0:T(8,128)(2,1)S(1)} %copy-done, bf16[128,1152]{1,0:T(8,128)(2,1)S(1)} %copy-done.1), custom_call_target="tpu_custom_call" | custom-call | flops 14495514624 | bytes 1769472 | tf_op jit(solution)/shard_map/pallas_call | solution.py:294
  56.2 0.8 %copy.10 = f32[128,1152]{1,0:T(8,128)} copy(f32[128,1152]{1,0:T(8,128)S(1)} %get-tuple-element.4) | data formatting | bytes 1179648
  57.0 0.8 %copy.11 = f32[128,1152]{1,0:T(8,128)} copy(f32[128,1152]{1,0:T(8,128)S(1)} %get-tuple-element.5) | data formatting | bytes 1179648
Async XLA Ops:
  1.9 1.0 %copy-start = (bf16[128,1152]{1,0:T(8,128)(2,1)S(1)}, bf16[128,1152]{1,0:T(8,128)(2,1)}, u32[]{:S(2)}) copy-start(bf16[128,1152]{1,0:T(8,128)(2,1)} %image_hbm.1) | copy-start | bytes 884740
  2.9 1.0 %copy-start.1 = (bf16[128,1152]{1,0:T(8,128)(2,1)S(1)}, bf16[128,1152]{1,0:T(8,128)(2,1)}, u32[]{:S(2)}) copy-start(bf16[128,1152]{1,0:T(8,128)(2,1)} %text_hbm.1) | copy-start | bytes 884740

commit v3 on v2

--- a/solution.py
+++ b/solution.py
@@ -272,8 +272,8 @@
         return inverse * (grads - normed * jnp.sum(normed * grads, axis=1, keepdims=True))
 
     text_inverse, text_norm = unit_rows(text_ref[...])
+    image_inverse, image_norm = unit_rows(image_ref[...])
     grad_text_ref[...] = finish(text_inverse, text_norm, total(1, 0))
-    image_inverse, image_norm = unit_rows(image_ref[...])
     grad_image_ref[...] = finish(image_inverse, image_norm, total(0, 0))
 
     for position in range(8):

time: 58 us -> 57.9 us (level)
  no operation moved by 1% of the time
where the time goes in v3:
time: 57.9 us; the launch traced here: 57.7 us
  Pallas kernels  52.2 us (90%)
  local copies, waits for them, and re-layouts  3.55 us (6%)
  between operations  1.94 us (3%)
    pallas_call x1, Pallas kernels, per_device(): pl.pallas_call(kernel, out_shape=(out, out), in_specs=[pl.BlockSpec(memor...  52.2 us
    unnamed x6, local copies, waits for them, and re-layouts  3.55 us

profile of v3, /device:TPU:8, one launch (start us, length us, event | category | flops | bytes accessed | tf_op | source)
XLA Modules:
  0.0 57.7 jit_solution(14093901632290614776)
XLA Ops:
  1.9 0.0 copy-start
  1.9 1.0 %copy-done = bf16[128,1152]{1,0:T(8,128)(2,1)S(1)} copy-done((bf16[128,1152]{1,0:T(8,128)(2,1)S(1)}, bf16[128,1152]{1,0:T(8,128)(2,1)}, u32[]{:S(2)}) %copy-start) | copy-done | bytes 294936
  2.9 0.0 copy-start.1
  2.9 1.0 %copy-done.1 = bf16[128,1152]{1,0:T(8,128)(2,1)S(1)} copy-done((bf16[128,1152]{1,0:T(8,128)(2,1)S(1)}, bf16[128,1152]{1,0:T(8,128)(2,1)}, u32[]{:S(2)}) %copy-start.1) | copy-done | bytes 294936
  3.8 52.2 %shard_map.59 = (f32[128,1152]{1,0:T(8,128)S(1)}, f32[128,1152]{1,0:T(8,128)S(1)}) custom-call(f32[1]{0:T(128)S(6)} %copy.8.scale_hbm, f32[1]{0:T(128)S(6)} %copy.9.bias_hbm, bf16[128,1152]{1,0:T(8,128)(2,1)S(1)} %copy-done, bf16[128,1152]{1,0:T(8,128)(2,1)S(1)} %copy-done.1), custom_call_target="tpu_custom_call" | custom-call | flops 14495514624 | bytes 1769472 | tf_op jit(solution)/shard_map/pallas_call | solution.py:294
  56.1 0.8 %copy.10 = f32[128,1152]{1,0:T(8,128)} copy(f32[128,1152]{1,0:T(8,128)S(1)} %get-tuple-element.4) | data formatting | bytes 1179648
  56.9 0.8 %copy.11 = f32[128,1152]{1,0:T(8,128)} copy(f32[128,1152]{1,0:T(8,128)S(1)} %get-tuple-element.5) | data formatting | bytes 1179648
Async XLA Ops:
  1.9 1.0 %copy-start = (bf16[128,1152]{1,0:T(8,128)(2,1)S(1)}, bf16[128,1152]{1,0:T(8,128)(2,1)}, u32[]{:S(2)}) copy-start(bf16[128,1152]{1,0:T(8,128)(2,1)} %image_hbm.1) | copy-start | bytes 884740
  2.9 1.0 %copy-start.1 = (bf16[128,1152]{1,0:T(8,128)(2,1)S(1)}, bf16[128,1152]{1,0:T(8,128)(2,1)}, u32[]{:S(2)}) copy-start(bf16[128,1152]{1,0:T(8,128)(2,1)} %text_hbm.1) | copy-start | bytes 884740
